TPU v7x, 32 devices: a whole 2x2x4 slice. The times are simulated.
32 devices in a mesh: mp: 2 (over core), heads: 8 (over z, y), tok: 2 (over x).
Axes of the slice: x: 2, y: 2, z: 4, core: 2. Of those that a mesh axis runs over, the one named last changes fastest.
Arguments:
- context: bfloat16 [2, 512, 8192], P('mp', None, 'heads'), may hold values from -6 to 6
- out_weight: bfloat16 [2, 8192, 8192], P('mp', 'heads', 'tok'), may hold values from -0.0625 to 0.0625
- skip_states: bfloat16 [2, 512, 8192], P(None, None, 'tok'), may hold values from -6 to 6
- gram_old: float32 [8192, 8192], P('tok', ('mp', 'heads')), may hold values from -1 to 3
- cross_old: float32 [8192, 8192], P('tok', ('mp', 'heads')), may hold values from -30 to 30
- map_old: float32 [8192, 8192], P('tok', ('mp', 'heads')), may hold values from -0.3 to 0.3
Outputs:
- gram_new: float32 [8192, 8192], P('tok', ('mp', 'heads'))
- cross_new: float32 [8192, 8192], P('tok', ('mp', 'heads'))
- map_new: float32 [8192, 8192], P('tok', ('mp', 'heads'))
- residual_new: float32 [8192, 8192], P('tok', ('mp', 'heads'))
All inputs are finite; a program needn't handle non-finite values.
Results may differ from a plain program's by a relative error of at most 0.03.
Values may be sent and summed in bfloat16 or wider, within the bound.
A program may use at most 256 MiB of HBM per device.

v0:
```python
import jax
import jax.numpy as jnp
from jax import lax
from jax.sharding import PartitionSpec as P

decay_keep = 0.75
ridge_weight = 0.1
f32, bf16 = (jnp.float32, jnp.bfloat16)
CHUNKS = 4


def dot(a, b):
    return jnp.dot(a, b, preferred_element_type=f32)


def token_inner(left, right):
    return lax.dot_general(left, right, (((0,), (0,)), ((), ())), preferred_element_type=f32)


def shifted(block, axis, shift):
    n = lax.axis_size(axis)
    return lax.ppermute(block, axis, [(i, (i + shift) % n) for i in range(n)])


def total_over(value, axis):
    n = lax.axis_size(axis)
    if n & n - 1:
        return lax.psum(value, axis)
    bit = 1
    while bit < n:
        value = value + lax.ppermute(value, axis, [(i, i ^ bit) for i in range(n)])
        bit *= 2
    return value


def sum_tok(value):
    n = lax.axis_size("tok")
    half = value.astype(bf16)
    for shift in range(1, n):
        value = value + shifted(half, "tok", shift).astype(f32)
    return value.astype(bf16)


def make_states(context, out_weight, skip_states, width):
    n_tok, n_heads, n_mp = (lax.axis_size(a) for a in ("tok", "heads", "mp"))
    t, h, k = (lax.axis_index(a) for a in ("tok", "heads", "mp"))
    tokens, features = skip_states.shape[1:]
    share = features // n_heads
    part = dot(context[0], out_weight[0]).astype(bf16)
    mine = lax.psum_scatter(part, "heads", scatter_dimension=1, tiled=True)
    skip = lax.dynamic_slice(skip_states, (k, 0, h * share), (1, tokens, share))[0]
    mine = (mine.astype(f32) + skip.astype(f32)).astype(bf16)
    other = lax.ppermute(mine, "mp", [(0, 1), (1, 0)])
    pair = jnp.stack([jnp.where(k == 0, mine, other), jnp.where(k == 0, other, mine)])
    if share == width and n_tok == n_mp == 2:
        away = lax.ppermute(pair, ("mp", "tok"), [(0, 1), (3, 2)])
        columns = jnp.where(k == t, pair, away)
        half = lax.dynamic_slice_in_dim(pair[0], k * (tokens // 2), tokens // 2, 0)
        rows = lax.all_gather(half, "heads", axis=1, tiled=True)
        rows_other = lax.ppermute(rows, "mp", [(0, 1), (1, 0)])
        first = jnp.where(k == 0, rows, rows_other)
        second = jnp.where(k == 0, rows_other, rows)
        source = jnp.concatenate([first, second], 0)
        return (source, columns[0], columns[1])
    both = lax.all_gather(pair, "heads", axis=2, tiled=True)
    whole = lax.all_gather(both, "tok", axis=2, tiled=True)
    columns = lax.dynamic_slice_in_dim(whole, (k * n_heads + h) * width, width, 2)
    return (both[0], columns[0], columns[1])


def per_device(context, out_weight, skip_states, gram_old, cross_old, map_old):
    n_tok = lax.axis_size("tok")
    t = lax.axis_index("tok")
    tokens = context.shape[1]
    height, width = gram_old.shape
    new_weight = (1.0 - decay_keep) / tokens
    step = height // CHUNKS
    cuts = [slice(c * step, (c + 1) * step) for c in range(CHUNKS)]
    map_half = map_old.astype(bf16)
    gram_old_half = gram_old.astype(bf16)
    panels = [
        lax.all_gather(gram_old_half[cut], ("mp", "heads"), axis=1, tiled=True) for cut in cuts
    ]
    maps = [map_half] + [shifted(map_half, "tok", s) for s in range(1, n_tok)]
    source, source_cols, target_cols = make_states(context, out_weight, skip_states, width)
    gram_new = decay_keep * gram_old + new_weight * token_inner(source, source_cols)
    cross_new = decay_keep * cross_old + new_weight * token_inner(source, target_cols)

    def panel_part(panel, s):
        owner = lax.rem(t - s + n_tok, n_tok)
        return lax.dynamic_slice_in_dim(panel, owner * height, height, 1)

    inner_map = sum_tok(dot(source, map_half))
    residuals, halves = ([], [])
    for cut, panel in zip(cuts, panels):
        product = sum((dot(panel_part(panel, s), maps[s]) for s in range(n_tok)))
        low_rank = token_inner(source[:, cut], inner_map)
        residual = (
            cross_new[cut]
            - decay_keep * product
            - new_weight * low_rank
            - ridge_weight * map_old[cut]
        )
        residuals.append(residual)
        halves.append(residual.astype(bf16))
    away = [[shifted(half, "tok", s) for half in halves] for s in range(1, n_tok)]
    inner_residual = sum_tok(sum((dot(source[:, cut], half) for cut, half in zip(cuts, halves))))
    blocks = [jnp.concatenate(halves, 0)] + [jnp.concatenate(a, 0) for a in away]
    applied, squares, mixed = ([], 0.0, 0.0)
    for cut, panel, residual in zip(cuts, panels, residuals):
        product = sum((dot(panel_part(panel, s), blocks[s]) for s in range(n_tok)))
        low_rank = token_inner(source[:, cut], inner_residual)
        value = decay_keep * product + new_weight * low_rank + ridge_weight * residual
        applied.append(value)
        squares = squares + jnp.sum(residual * residual)
        mixed = mixed + jnp.sum(residual * value)
    totals = jnp.stack([squares, mixed])
    for axis in ("mp", "tok", "heads"):
        totals = total_over(totals, axis)
    step_size = totals[0] / totals[1]
    residual = jnp.concatenate(residuals, 0)
    return (
        gram_new,
        cross_new,
        map_old + step_size * residual,
        residual - step_size * jnp.concatenate(applied, 0),
    )


def solution(mesh):
    block = P("tok", ("mp", "heads"))
    placed = (
        P("mp", None, "heads"),
        P("mp", "heads", "tok"),
        P(None, None, "tok"),
        block,
        block,
        block,
    )
    return jax.shard_map(
        per_device, mesh=mesh, in_specs=placed, out_specs=(block,) * 4, check_vma=False
    )
```

profile of v0, /device:TPU:0, one launch (start us, length us, event | category | flops | bytes accessed | tf_op | source)
XLA Modules:
  0.0 842.1 jit_solution(6807376808990272788)
XLA Ops:
  8.4 9.4 %fusion.35 = bf16[512,4096]{1,0:T(8,128)(2,1)} fusion(bf16[1,1024,4096]{2,1,0:T(8,128)(2,1)} %param.7, bf16[1,512,1024]{2,1,0:T(8,128)(2,1)S(1)} %copy-done), kind=kOutput, calls=%fused_computation.49 | convolution fusion | flops 4297064448 | bytes 13631488 | tf_op jit(solution)/shard_map/dot_general | solution.py:13
  17.9 91.3 %reduce-scatter.2.cloned.1.call-done = bf16[512,512]{1,0:T(8,128)(2,1)} async-done(((bf16[512,4096]{1,0:T(8,128)(2,1)}), bf16[512,512]{1,0:T(8,128)(2,1)}) %reduce-scatter.2.cloned.1.call-update) | async-done | bytes 524304 | tf_op jit(solution)/shard_map/reduce_scatter | solution.py:50
  113.3 3.9 convert_element_type.56
  121.1 43.2 %all-gather.6.cloned.1.call-done = bf16[256,4096]{1,0:T(8,128)(2,1)} async-done(((bf16[256,512]{1,0:T(8,128)(2,1)}), bf16[256,4096]{1,0:T(8,128)(2,1)}) %all-gather.6.cloned.1.call-update) | async-done | bytes 2097168 | tf_op jit(solution)/shard_map/all_gather | solution.py:59
  164.4 3.4 collective-permute-start.2
  167.8 6.0 convert_element_type.57
  173.8 11.4 %collective-permute-done.2 = bf16[2,512,512]{2,1,0:T(8,128)(2,1)S(1)} collective-permute-done((bf16[2,512,512]{2,1,0:T(8,128)(2,1)S(1)}, bf16[2,512,512]{2,1,0:T(8,128)(2,1)S(1)}, u32[]{:S(2)}, u32[]{:S(2)}) %collective-permute-start.2) | collective-permute-done | bytes 1048608 | tf_op jit(solution)/shard_map/ppermute | solution.py:56
  185.3 2.6 broadcast_select_fusion.1
  188.0 5.4 fusion.79
  193.4 2.6 collective-permute-start.4
  196.0 5.0 multiply_add_fusion.2
  201.0 4.9 multiply_add_fusion.1
  207.7 73.5 %collective-permute-done.4 = bf16[512,512]{1,0:T(8,128)(2,1)S(1)} collective-permute-done((bf16[512,512]{1,0:T(8,128)(2,1)S(1)}, bf16[512,512]{1,0:T(8,128)(2,1)S(1)}, u32[]{:S(2)}, u32[]{:S(2)}) %collective-permute-start.4) | collective-permute-done | bytes 524320 | tf_op jit(solution)/shard_map/ppermute | solution.py:22
  281.4 14.3 %all-gather.10.cloned.1.call-done = bf16[1024,8192]{1,0:T(8,128)(2,1)} async-done(((bf16[1024,512]{1,0:T(8,128)(2,1)}), bf16[1024,8192]{1,0:T(8,128)(2,1)}) %all-gather.10.cloned.1.call-update) | async-done | bytes 16777232 | tf_op jit(solution)/shard_map/all_gather | solution.py:82
  295.7 8.3 fusion.25
  305.9 6.6 fusion.21
  312.5 5.0 fusion.82
  318.9 107.4 %all-gather.12.cloned.1.call-done = bf16[1024,8192]{1,0:T(8,128)(2,1)} async-done(((bf16[1024,512]{1,0:T(8,128)(2,1)}), bf16[1024,8192]{1,0:T(8,128)(2,1)}) %all-gather.12.cloned.1.call-update) | async-done | bytes 16777232 | tf_op jit(solution)/shard_map/all_gather | solution.py:82
  426.4 8.3 fusion.13
  436.6 6.7 fusion.17
  443.3 5.0 fusion.81
  449.7 107.4 %all-gather.14.cloned.1.call-done = bf16[1024,8192]{1,0:T(8,128)(2,1)} async-done(((bf16[1024,512]{1,0:T(8,128)(2,1)}), bf16[1024,8192]{1,0:T(8,128)(2,1)}) %all-gather.14.cloned.1.call-update) | async-done | bytes 16777232 | tf_op jit(solution)/shard_map/all_gather | solution.py:82
  557.1 8.5 %fusion.5 = f32[1024,512]{1,0:T(8,128)S(1)} fusion(bf16[4096,512]{1,0:T(8,128)(2,1)} %collective-permute-done.3, bf16[1024,8192]{1,0:T(8,128)(2,1)} %all-gather.14.cloned.1.call-done, s32[]{:T(128)S(6)} %select_n.73), kind=kOutput, calls=%fused_computation.10 | convolution fusion | flops 4294967296 | bytes 14680068 | tf_op jit(solution)/shard_map/dot_general | solution.py:13
  567.2 6.7 fusion.9
  574.0 5.3 fusion.80
  580.7 2.9 fusion.85
  583.6 2.9 fusion.86
  586.6 2.9 fusion.87
  589.5 98.3 %all-gather.8.cloned.1.call-done = bf16[1024,8192]{1,0:T(8,128)(2,1)} async-done(((bf16[1024,512]{1,0:T(8,128)(2,1)}), bf16[1024,8192]{1,0:T(8,128)(2,1)}) %all-gather.8.cloned.1.call-update) | async-done | bytes 16777232 | tf_op jit(solution)/shard_map/all_gather | solution.py:82
  687.8 8.3 fusion.29
  697.2 6.6 fusion.33
  703.9 3.6 fusion.83
  710.3 9.2 %fusion.31 = f32[1024,512]{1,0:T(8,128)S(1)} fusion(bf16[1024,8192]{1,0:T(8,128)(2,1)} %all-gather.8.cloned.1.call-done, s32[]{:T(128)S(6)} %select_n.72, bf16[1024,512]{1,0:T(8,128)(2,1)} %get-tuple-element.29, bf16[1024,512]{1,0:T(8,128)(2,1)} %get-tuple-element.31, bf16[1024,512]{1,0:T(8,128)(2,1)} %get-tuple-element.33, ...), kind=kOutput, calls=%fused_computation.36 | convolution fusion | flops 4311744512 | bytes 14680068 | tf_op jit(solution)/shard_map/dot_general | solution.py:13
  719.6 8.8 %fusion.23 = f32[1024,512]{1,0:T(8,128)S(1)} fusion(bf16[1024,8192]{1,0:T(8,128)(2,1)} %all-gather.10.cloned.1.call-done, s32[]{:T(128)S(6)} %select_n.72, bf16[1024,512]{1,0:T(8,128)(2,1)} %get-tuple-element.29, bf16[1024,512]{1,0:T(8,128)(2,1)} %get-tuple-element.31, bf16[1024,512]{1,0:T(8,128)(2,1)} %get-tuple-element.33, ...), kind=kOutput, calls=%fused_computation.28 | convolution fusion | flops 4311744512 | bytes 14680068 | tf_op jit(solution)/shard_map/dot_general | solution.py:13
  728.4 10.0 %fusion.15 = f32[1024,512]{1,0:T(8,128)} fusion(bf16[1024,8192]{1,0:T(8,128)(2,1)} %all-gather.12.cloned.1.call-done, s32[]{:T(128)S(6)} %select_n.72, bf16[1024,512]{1,0:T(8,128)(2,1)} %get-tuple-element.29, bf16[1024,512]{1,0:T(8,128)(2,1)} %get-tuple-element.31, bf16[1024,512]{1,0:T(8,128)(2,1)} %get-tuple-element.33, ...), kind=kOutput, calls=%fused_computation.20 | convolution fusion | flops 4311744512 | bytes 14680068 | tf_op jit(solution)/shard_map/dot_general | solution.py:13
  738.4 10.1 %fusion.7 = f32[1024,512]{1,0:T(8,128)} fusion(bf16[1024,8192]{1,0:T(8,128)(2,1)} %all-gather.14.cloned.1.call-done, s32[]{:T(128)S(6)} %select_n.72, bf16[1024,512]{1,0:T(8,128)(2,1)} %get-tuple-element.29, bf16[1024,512]{1,0:T(8,128)(2,1)} %get-tuple-element.31, bf16[1024,512]{1,0:T(8,128)(2,1)} %get-tuple-element.33, ...), kind=kOutput, calls=%fused_computation.12 | convolution fusion | flops 4311744512 | bytes 14680068 | tf_op jit(solution)/shard_map/dot_general | solution.py:13
  752.7 8.6 %fusion.27 = f32[1024,512]{1,0:T(8,128)S(1)} fusion(bf16[4096,512]{1,0:T(8,128)(2,1)S(1)} %constant_dynamic-update-slice_fusion, bf16[1024,8192]{1,0:T(8,128)(2,1)} %all-gather.8.cloned.1.call-done, s32[]{:T(128)S(6)} %select_n.73), kind=kOutput, calls=%fused_computation.32 | convolution fusion | flops 4294967296 | bytes 14680068 | tf_op jit(solution)/shard_map/dot_general | solution.py:13
  761.4 3.0 multiply_reduce_fusion.7
  764.4 7.1 fusion.19
  771.5 3.2 multiply_reduce_fusion.6
  776.0 8.3 fusion.11
  784.3 3.0 multiply_reduce_fusion.5
  788.0 8.3 fusion.3
  796.3 3.1 multiply_reduce_fusion.4
  808.9 2.1 collective-permute-done.12
  811.0 3.5 collective-permute-done.13
  816.1 2.9 collective-permute-done.14
  820.9 14.1 %fusion = (f32[4096,512]{1,0:T(8,128)}, f32[4096,512]{1,0:T(8,128)}) fusion(f32[1024,512]{1,0:T(8,128)} %get-tuple-element.42, f32[1024,512]{1,0:T(8,128)} %get-tuple-element.41, f32[1024,512]{1,0:T(8,128)} %get-tuple-element.40, f32[1024,512]{1,0:T(8,128)} %get-tuple-element.39, f32[1024,512]{1,0:T(8,128)} %get-tuple-element.30, ...), kind=kLoop, calls=%fused_computation.2 | loop fusion | flops 20971520 | bytes 41943044 | tf_op jit(solution)/shard_map/sub | solution.py:126
  (118 shorter events, 37.9 us)
Async XLA Ops:
  7.2 102.0 %reduce-scatter.2.cloned.1.call-start = ((), (), s32[]{:S(2)}) async-start(), calls=%async_computation.1 | async-start | bytes 4718592 | tf_op jit(solution)/shard_map/reduce_scatter | solution.py:50
  17.8 146.5 %all-gather.6.cloned.1.call-start = ((), (), s32[]{:S(2)}) async-start(), calls=%async_computation.2 | async-start | bytes 2359296 | tf_op jit(solution)/shard_map/all_gather | solution.py:59
  110.5 2.0 collective-permute-start
  113.3 182.4 %all-gather.10.cloned.1.call-start = ((), (), s32[]{:S(2)}) async-start(), calls=%async_computation.4 | async-start | bytes 17825792 | tf_op jit(solution)/shard_map/all_gather | solution.py:82
  119.4 307.0 %all-gather.12.cloned.1.call-start = ((), (), s32[]{:S(2)}) async-start(), calls=%async_computation.5 | async-start | bytes 17825792 | tf_op jit(solution)/shard_map/all_gather | solution.py:82
  119.9 437.1 %all-gather.14.cloned.1.call-start = ((), (), s32[]{:S(2)}) async-start(), calls=%async_computation.6 | async-start | bytes 17825792 | tf_op jit(solution)/shard_map/all_gather | solution.py:82
  120.5 567.2 %all-gather.8.cloned.1.call-start = ((), (), s32[]{:S(2)}) async-start(), calls=%async_computation.3 | async-start | bytes 17825792 | tf_op jit(solution)/shard_map/all_gather | solution.py:82
  164.3 21.0 %collective-permute-start.1 = (bf16[256,4096]{1,0:T(8,128)(2,1)}, bf16[256,4096]{1,0:T(8,128)(2,1)}, u32[]{:S(2)}, u32[]{:S(2)}) collective-permute-start(bf16[256,4096]{1,0:T(8,128)(2,1)} %all-gather.6.cloned.1.call-done), channel_id=1, source_target_pairs={{0,16},{16,0},{1,17},{17,1},{2,18},{18,2},{3,19},{19,3},{4,20},{20... | collective-permute-start | bytes 6291464 | tf_op jit(solution)/shard_map/ppermute | solution.py:60
  164.4 20.8 %collective-permute-start.2 = (bf16[2,512,512]{2,1,0:T(8,128)(2,1)S(1)}, bf16[2,512,512]{2,1,0:T(8,128)(2,1)S(1)}, u32[]{:S(2)}, u32[]{:S(2)}) collective-permute-start(bf16[2,512,512]{2,1,0:T(8,128)(2,1)S(1)} %pad_maximum_fusion.6), channel_id=1, source_target_pairs={{0,1},{17,16},{2,3},{19,18},{4,5},{21,20},{6,7},{23,22},{8,9},{25,... | collective-permute-start | bytes 3145736 | tf_op jit(solution)/shard_map/ppermute | solution.py:56
  173.8 130.2 %collective-permute-start.3 = (bf16[4096,512]{1,0:T(8,128)(2,1)}, bf16[4096,512]{1,0:T(8,128)(2,1)}, u32[]{:S(2)}, u32[]{:S(2)}) collective-permute-start(bf16[4096,512]{1,0:T(8,128)(2,1)} %convert_element_type.57), channel_id=1, source_target_pairs={{0,1},{1,0},{2,3},{3,2},{4,5},{5,4},{6,7},{7,6},{8,9},{9,8},{10,11... | collective-permute-start | bytes 12582920 | tf_op jit(solution)/shard_map/ppermute | solution.py:22
  185.3 10.7 %slice-start = ((s8[8388608]{0:T(1024)(128)(4,1)}), s8[4194304]{0:T(1024)(128)(4,1)S(1)}, s32[]{:S(2)}) async-start(s8[8388608]{0:T(1024)(128)(4,1)} %bitcast.57), calls=%async_computation.7 | async-start | bytes 8388608
  188.0 17.9 %copy-start.2 = (bf16[256,4096]{1,0:T(8,128)(2,1)}, bf16[256,4096]{1,0:T(8,128)(2,1)S(1)}, u32[]{:S(2)}) copy-start(bf16[256,4096]{1,0:T(8,128)(2,1)S(1)} %get-tuple-element.22) | copy-start | bytes 6291460
  188.0 8.0 slice-start.1
  193.4 7.6 slice-start.2
  193.4 7.6 slice-start.3
  193.4 87.8 %collective-permute-start.4 = (bf16[512,512]{1,0:T(8,128)(2,1)S(1)}, bf16[512,512]{1,0:T(8,128)(2,1)S(1)}, u32[]{:S(2)}, u32[]{:S(2)}) collective-permute-start(bf16[512,512]{1,0:T(8,128)(2,1)S(1)} %get-tuple-element.27), channel_id=1, source_target_pairs={{0,1},{1,0},{2,3},{3,2},{4,5},{5,4},{6,7},{7,6},{8,9},{9,8},{10,11... | collective-permute-start | bytes 1572872 | tf_op jit(solution)/shard_map/ppermute | solution.py:22
  295.7 10.2 %copy-start.24 = (bf16[1024,8192]{1,0:T(8,128)(2,1)S(1)}, bf16[1024,8192]{1,0:T(8,128)(2,1)}, u32[]{:S(2)}) copy-start(bf16[1024,8192]{1,0:T(8,128)(2,1)} %all-gather.10.cloned.1.call-done) | copy-start | bytes 50331652
  304.0 8.5 %copy-start.13 = (bf16[512,1024]{1,0:T(8,128)(2,1)S(1)}, bf16[512,1024]{1,0:T(8,128)(2,1)}, u32[]{:S(2)}) copy-start(bf16[512,1024]{1,0:T(8,128)(2,1)} %get-tuple-element.18) | copy-start | bytes 3145732
  317.5 431.3 %collective-permute-start.6 = (bf16[1024,512]{1,0:T(8,128)(2,1)}, bf16[1024,512]{1,0:T(8,128)(2,1)}, u32[]{:S(2)}, u32[]{:S(2)}) collective-permute-start(bf16[1024,512]{1,0:T(8,128)(2,1)} %get-tuple-element.33), channel_id=1, source_target_pairs={{0,1},{1,0},{2,3},{3,2},{4,5},{5,4},{6,7},{7,6},{8,9},{9,8},{10,11... | collective-permute-start | bytes 3145736 | tf_op jit(solution)/shard_map/ppermute | solution.py:22
  426.4 10.2 %copy-start.23 = (bf16[1024,8192]{1,0:T(8,128)(2,1)S(1)}, bf16[1024,8192]{1,0:T(8,128)(2,1)}, u32[]{:S(2)}) copy-start(bf16[1024,8192]{1,0:T(8,128)(2,1)} %all-gather.12.cloned.1.call-done) | copy-start | bytes 50331652
  436.6 6.7 copy-start.10
  448.3 301.8 %collective-permute-start.7 = (bf16[1024,512]{1,0:T(8,128)(2,1)}, bf16[1024,512]{1,0:T(8,128)(2,1)}, u32[]{:S(2)}, u32[]{:S(2)}) collective-permute-start(bf16[1024,512]{1,0:T(8,128)(2,1)} %get-tuple-element.31), channel_id=1, source_target_pairs={{0,1},{1,0},{2,3},{3,2},{4,5},{5,4},{6,7},{7,6},{8,9},{9,8},{10,11... | collective-permute-start | bytes 3145736 | tf_op jit(solution)/shard_map/ppermute | solution.py:22
  557.1 10.2 %copy-start.22 = (bf16[1024,8192]{1,0:T(8,128)(2,1)S(1)}, bf16[1024,8192]{1,0:T(8,128)(2,1)}, u32[]{:S(2)}) copy-start(bf16[1024,8192]{1,0:T(8,128)(2,1)} %all-gather.14.cloned.1.call-done) | copy-start | bytes 50331652
  567.2 6.7 copy-start.8
  574.0 6.7 copy-start.14
  574.0 9.7 %copy-start.11 = (bf16[512,1024]{1,0:T(8,128)(2,1)S(1)}, bf16[512,1024]{1,0:T(8,128)(2,1)}, u32[]{:S(2)}) copy-start(bf16[512,1024]{1,0:T(8,128)(2,1)} %get-tuple-element.19) | copy-start | bytes 3145732
  579.3 172.2 %collective-permute-start.8 = (bf16[1024,512]{1,0:T(8,128)(2,1)}, bf16[1024,512]{1,0:T(8,128)(2,1)}, u32[]{:S(2)}, u32[]{:S(2)}) collective-permute-start(bf16[1024,512]{1,0:T(8,128)(2,1)} %get-tuple-element.29), channel_id=1, source_target_pairs={{0,1},{1,0},{2,3},{3,2},{4,5},{5,4},{6,7},{7,6},{8,9},{9,8},{10,11... | collective-permute-start | bytes 3145736 | tf_op jit(solution)/shard_map/ppermute | solution.py:22
  687.8 9.4 %copy-start.25 = (bf16[1024,8192]{1,0:T(8,128)(2,1)S(1)}, bf16[1024,8192]{1,0:T(8,128)(2,1)}, u32[]{:S(2)}) copy-start(bf16[1024,8192]{1,0:T(8,128)(2,1)} %all-gather.8.cloned.1.call-done) | copy-start | bytes 50331652
  697.2 6.7 copy-start.3
  703.8 5.1 copy-start.18
  707.4 53.9 %copy-start.7 = (f32[1024,512]{1,0:T(8,128)}, f32[1024,512]{1,0:T(8,128)S(1)}, u32[]{:S(2)}) copy-start(f32[1024,512]{1,0:T(8,128)S(1)} %get-tuple-element.36) | copy-start | bytes 6291460
  707.4 41.3 %collective-permute-start.5 = (bf16[1024,512]{1,0:T(8,128)(2,1)S(1)}, bf16[1024,512]{1,0:T(8,128)(2,1)S(1)}, u32[]{:S(2)}, u32[]{:S(2)}) collective-permute-start(bf16[1024,512]{1,0:T(8,128)(2,1)S(1)} %get-tuple-element.35), channel_id=1, source_target_pairs={{0,1},{1,0},{2,3},{3,2},{4,5},{5,4},{6,7},{7,6},{8,9},{9,8},{10,11... | collective-permute-start | bytes 3145736 | tf_op jit(solution)/shard_map/ppermute | solution.py:22
  709.7 38.8 %collective-permute-start.9 = (bf16[512,512]{1,0:T(8,128)(2,1)S(1)}, bf16[512,512]{1,0:T(8,128)(2,1)S(1)}, u32[]{:S(2)}, u32[]{:S(2)}) collective-permute-start(bf16[512,512]{1,0:T(8,128)(2,1)S(1)} %get-tuple-element.37), channel_id=1, source_target_pairs={{0,1},{1,0},{2,3},{3,2},{4,5},{5,4},{6,7},{7,6},{8,9},{9,8},{10,11... | collective-permute-start | bytes 1572872 | tf_op jit(solution)/shard_map/ppermute | solution.py:22
  752.7 11.7 %copy-start.21 = (bf16[4096,512]{1,0:T(8,128)(2,1)}, bf16[4096,512]{1,0:T(8,128)(2,1)S(1)}, u32[]{:S(2)}) copy-start(bf16[4096,512]{1,0:T(8,128)(2,1)S(1)} %constant_dynamic-update-slice_fusion) | copy-start | bytes 12582916
  764.4 7.1 copy-start.4
  764.4 7.1 copy-start.15
  775.9 8.3 copy-start.5
  775.9 8.3 copy-start.12
  776.0 8.3 copy-start.17
  788.0 8.3 copy-start.6
  788.0 8.3 copy-start.9
  788.0 8.3 copy-start.16
  802.6 1.1 collective-permute-start.10
  803.9 3.5 collective-permute-start.11
  807.5 3.5 collective-permute-start.12
  811.0 3.5 collective-permute-start.13
  814.6 4.4 collective-permute-start.14
  820.9 14.1 %copy-start.1 = (bf16[1,512,1024]{2,1,0:T(8,128)(2,1)S(1)}, bf16[1,512,1024]{2,1,0:T(8,128)(2,1)}, u32[]{:S(2)}) copy-start(bf16[1,512,1024]{2,1,0:T(8,128)(2,1)} %param.6) | copy-start | bytes 3145732
  (3 other events, 11.5 us)
Sparse Core Ops, SparseCore 0:
  17.9 91.1 reduce-scatter.1
  113.4 50.8 all-gather.5
  167.1 128.5 all-gather.9
  297.8 128.5 all-gather.11
  428.5 128.5 all-gather.13
  559.2 128.5 all-gather.7
where the time goes:
time: 848 us; the launch traced here: 842 us
  waiting for transfers between devices  562 us (66%)
  matrix products  196 us (23%)
  other arithmetic  30.7 us (4%)
  between operations  21.2 us (2%)
  starting transfers between devices  17.1 us (2%)
  local copies, waits for them, and re-layouts  15.3 us (2%)
    all_gather x4, waiting for transfers between devices, per_device(): lax.all_gather(gram_old_half[cut], ('mp', 'heads'), axis=1, tiled=True)  327 us
    dot_general x22, matrix products, dot(): return jnp.dot(a, b, preferred_element_type=f32)  155 us
    reduce_scatter x1, waiting for transfers between devices, make_states(): mine = lax.psum_scatter(part, 'heads', scatter_dimension=1, tiled=True)  91.3 us
    ppermute x7, waiting for transfers between devices, shifted(): return lax.ppermute(block, axis, [(i, (i + shift) % n) for i in range(n)])  73.5 us
    all_gather x1, waiting for transfers between devices, make_states(): rows = lax.all_gather(half, 'heads', axis=1, tiled=True)  43.2 us
    dot_general x10, matrix products, token_inner(): lax.dot_general(left, right, (((0,), (0,)), ((), ())), preferred_element_...  41.2 us
  transfers between devices with their start and end apart: 21, of which 14 were waited for; matrix products, arithmetic and copies ran while one was open for 19% of the time, Pallas kernels for 0%

commit v1 on v0

--- a/solution.py
+++ b/solution.py
@@ -7,6 +7,18 @@
 ridge_weight = 0.1
 f32, bf16 = (jnp.float32, jnp.bfloat16)
 CHUNKS = 4
+
+
+def doubled_up(array, axis, dim):
+    ways, here = (lax.axis_size(axis), lax.axis_index(axis))
+    grown, reach = (array, 1)
+    while reach < ways:
+        theirs = lax.ppermute(grown, axis, [(d, d ^ reach) for d in range(ways)])
+        mine_first = jnp.concatenate([grown, theirs], axis=dim)
+        theirs_first = jnp.concatenate([theirs, grown], axis=dim)
+        grown = jnp.where(here & reach == 0, mine_first, theirs_first)
+        reach = 2 * reach
+    return grown
 
 
 def dot(a, b):
@@ -56,7 +68,7 @@
         away = lax.ppermute(pair, ("mp", "tok"), [(0, 1), (3, 2)])
         columns = jnp.where(k == t, pair, away)
         half = lax.dynamic_slice_in_dim(pair[0], k * (tokens // 2), tokens // 2, 0)
-        rows = lax.all_gather(half, "heads", axis=1, tiled=True)
+        rows = doubled_up(half, "heads", 1)
         rows_other = lax.ppermute(rows, "mp", [(0, 1), (1, 0)])
         first = jnp.where(k == 0, rows, rows_other)
         second = jnp.where(k == 0, rows_other, rows)

time: 848 us -> 781 us (0.921)
  waiting for transfers between devices: 562 us -> 481 us
  starting transfers between devices: 17.1 us -> 25.6 us
    all_gather x4, waiting for transfers between devices: 327 us -> 81.7 us  [per_device(): lax.all_gather(gram_old_half[cut], ('mp', 'heads'), axis=1, tiled=True)]
    ppermute x0 -> x3, waiting for transfers between devices: none -> 141 us  [doubled_up(): theirs = lax.ppermute(grown, axis, [(d, d ^ reach) for d in range(ways)])]
    reduce_scatter x1, waiting for transfers between devices: 91.3 us -> 160 us  [make_states(): mine = lax.psum_scatter(part, 'heads', scatter_dimension=1, tiled=True)]
    all_gather x1 -> x0, waiting for transfers between devices: 43.2 us -> none  [make_states(): rows = lax.all_gather(half, 'heads', axis=1, tiled=True)]
  transfers between devices with their start and end apart: 21 -> 23, of which waited for: 14 -> 13; matrix products, arithmetic and copies ran while one was open for 19% -> 22% of each run, Pallas kernels for 0% -> 0%
where the time goes in v1:
time: 781 us; the launch traced here: 774 us
  waiting for transfers between devices  481 us (62%)
  matrix products  197 us (25%)
  other arithmetic  34.9 us (4%)
  starting transfers between devices  25.6 us (3%)
  between operations  23 us (3%)
  local copies, waits for them, and re-layouts  12.5 us (2%)
    reduce_scatter x1, waiting for transfers between devices, make_states(): mine = lax.psum_scatter(part, 'heads', scatter_dimension=1, tiled=True)  160 us
    dot_general x22, matrix products, dot(): return jnp.dot(a, b, preferred_element_type=f32)  156 us
    ppermute x3, waiting for transfers between devices, doubled_up(): theirs = lax.ppermute(grown, axis, [(d, d ^ reach) for d in range(ways)])  141 us
    all_gather x4, waiting for transfers between devices, per_device(): lax.all_gather(gram_old_half[cut], ('mp', 'heads'), axis=1, tiled=True)  81.7 us
    ppermute x7, waiting for transfers between devices, shifted(): return lax.ppermute(block, axis, [(i, (i + shift) % n) for i in range(n)])  72.2 us
    dot_general x10, matrix products, token_inner(): lax.dot_general(left, right, (((0,), (0,)), ((), ())), preferred_element_...  41.3 us
  transfers between devices with their start and end apart: 23, of which 13 were waited for; matrix products, arithmetic and copies ran while one was open for 22% of the time, Pallas kernels for 0%

profile of v1, /device:TPU:0, one launch (start us, length us, event | category | flops | bytes accessed | tf_op | source)
XLA Modules:
  0.0 774.5 jit_solution(13167531466207700208)
XLA Ops:
  9.2 9.4 %fusion.35 = bf16[512,4096]{1,0:T(8,128)(2,1)} fusion(bf16[1,1024,4096]{2,1,0:T(8,128)(2,1)} %param.7, bf16[1,512,1024]{2,1,0:T(8,128)(2,1)S(1)} %copy-done), kind=kOutput, calls=%fused_computation.49 | convolution fusion | flops 4297064448 | bytes 13631488 | tf_op jit(solution)/shard_map/dot_general | solution.py:25
  18.7 3.9 convert_element_type.56
  26.7 160.2 %reduce-scatter.2.cloned.1.call-done = bf16[512,512]{1,0:T(8,128)(2,1)} async-done(((bf16[512,4096]{1,0:T(8,128)(2,1)}), bf16[512,512]{1,0:T(8,128)(2,1)}) %reduce-scatter.2.cloned.1.call-update) | async-done | bytes 524304 | tf_op jit(solution)/shard_map/reduce_scatter | solution.py:62
  191.8 10.2 %collective-permute-done.1 = bf16[256,512]{1,0:T(8,128)(2,1)S(1)} collective-permute-done((bf16[256,512]{1,0:T(8,128)(2,1)S(1)}, bf16[256,512]{1,0:T(8,128)(2,1)S(1)}, u32[]{:S(2)}, u32[]{:S(2)}) %collective-permute-start.1) | collective-permute-done | bytes 262176 | tf_op jit(solution)/shard_map/ppermute | solution.py:16
  203.8 29.6 %collective-permute-done.2 = bf16[256,1024]{1,0:T(8,128)(2,1)S(1)} collective-permute-done((bf16[256,1024]{1,0:T(8,128)(2,1)S(1)}, bf16[256,1024]{1,0:T(8,128)(2,1)S(1)}, u32[]{:S(2)}, u32[]{:S(2)}) %collective-permute-start.2) | collective-permute-done | bytes 524320 | tf_op jit(solution)/shard_map/ppermute | solution.py:16
  233.8 2.5 collective-permute-start.3
  236.3 101.2 %collective-permute-done.3 = bf16[256,2048]{1,0:T(8,128)(2,1)} collective-permute-done((bf16[256,2048]{1,0:T(8,128)(2,1)S(1)}, bf16[256,2048]{1,0:T(8,128)(2,1)}, u32[]{:S(2)}, u32[]{:S(2)}) %collective-permute-start.3) | collective-permute-done | bytes 1048608 | tf_op jit(solution)/shard_map/ppermute | solution.py:16
  337.4 3.0 maximum_select_fusion
  341.7 4.9 collective-permute-start.5
  346.6 5.9 convert_element_type.57
  352.5 10.7 %collective-permute-done.5 = bf16[2,512,512]{2,1,0:T(8,128)(2,1)} collective-permute-done((bf16[2,512,512]{2,1,0:T(8,128)(2,1)}, bf16[2,512,512]{2,1,0:T(8,128)(2,1)}, u32[]{:S(2)}, u32[]{:S(2)}) %collective-permute-start.5) | collective-permute-done | bytes 1048608 | tf_op jit(solution)/shard_map/ppermute | solution.py:68
  365.8 5.6 fusion.79
  371.4 3.9 collective-permute-start.7
  375.3 5.0 multiply_add_fusion.2
  380.3 4.9 multiply_add_fusion.1
  387.1 72.2 %collective-permute-done.7 = bf16[512,512]{1,0:T(8,128)(2,1)S(1)} collective-permute-done((bf16[512,512]{1,0:T(8,128)(2,1)S(1)}, bf16[512,512]{1,0:T(8,128)(2,1)S(1)}, u32[]{:S(2)}, u32[]{:S(2)}) %collective-permute-start.7) | collective-permute-done | bytes 524320 | tf_op jit(solution)/shard_map/ppermute | solution.py:34
  459.5 8.6 %fusion.25 = f32[1024,512]{1,0:T(8,128)S(1)} fusion(bf16[4096,512]{1,0:T(8,128)(2,1)} %convert_element_type.57, bf16[1024,8192]{1,0:T(8,128)(2,1)} %all-gather.7.cloned.1.call-done, s32[]{:T(128)S(6)} %select_n.100), kind=kOutput, calls=%fused_computation.30 | convolution fusion | flops 4294967296 | bytes 14680068 | tf_op jit(solution)/shard_map/dot_general | solution.py:25
  469.4 6.5 fusion.21
  475.9 5.1 fusion.82
  481.0 2.3 collective-permute-start.9
  483.3 9.1 %fusion.13 = f32[1024,512]{1,0:T(8,128)S(1)} fusion(bf16[4096,512]{1,0:T(8,128)(2,1)} %collective-permute-done.6, bf16[1024,8192]{1,0:T(8,128)(2,1)} %all-gather.9.cloned.1.call-done, s32[]{:T(128)S(6)} %select_n.101), kind=kOutput, calls=%fused_computation.18 | convolution fusion | flops 4294967296 | bytes 14680068 | tf_op jit(solution)/shard_map/dot_general | solution.py:25
  493.5 6.6 fusion.17
  500.2 5.1 fusion.81
  505.4 8.5 %fusion.5 = f32[1024,512]{1,0:T(8,128)S(1)} fusion(bf16[4096,512]{1,0:T(8,128)(2,1)} %collective-permute-done.6, bf16[1024,8192]{1,0:T(8,128)(2,1)} %all-gather.11.cloned.1.call-done, s32[]{:T(128)S(6)} %select_n.101), kind=kOutput, calls=%fused_computation.10 | convolution fusion | flops 4294967296 | bytes 14680068 | tf_op jit(solution)/shard_map/dot_general | solution.py:25
  514.9 6.6 fusion.9
  521.5 5.3 fusion.80
  528.8 2.9 fusion.85
  531.7 2.9 fusion.86
  534.6 3.0 fusion.87
  537.6 81.7 %all-gather.5.cloned.1.call-done = bf16[1024,8192]{1,0:T(8,128)(2,1)} async-done(((bf16[1024,512]{1,0:T(8,128)(2,1)}), bf16[1024,8192]{1,0:T(8,128)(2,1)}) %all-gather.5.cloned.1.call-update) | async-done | bytes 16777232 | tf_op jit(solution)/shard_map/all_gather | solution.py:94
  619.3 8.3 %fusion.29 = f32[1024,512]{1,0:T(8,128)S(1)} fusion(bf16[4096,512]{1,0:T(8,128)(2,1)} %collective-permute-done.6, bf16[1024,8192]{1,0:T(8,128)(2,1)} %all-gather.5.cloned.1.call-done, s32[]{:T(128)S(6)} %select_n.101), kind=kOutput, calls=%fused_computation.34 | convolution fusion | flops 4294967296 | bytes 14680068 | tf_op jit(solution)/shard_map/dot_general | solution.py:25
  628.7 6.7 fusion.33
  635.4 3.5 fusion.83
  641.9 9.2 %fusion.31 = f32[1024,512]{1,0:T(8,128)S(1)} fusion(bf16[1024,8192]{1,0:T(8,128)(2,1)} %all-gather.5.cloned.1.call-done, s32[]{:T(128)S(6)} %select_n.100, bf16[1024,512]{1,0:T(8,128)(2,1)} %get-tuple-element.29, bf16[1024,512]{1,0:T(8,128)(2,1)} %get-tuple-element.31, bf16[1024,512]{1,0:T(8,128)(2,1)} %get-tuple-element.33, ...), kind=kOutput, calls=%fused_computation.36 | convolution fusion | flops 4311744512 | bytes 14680068 | tf_op jit(solution)/shard_map/dot_general | solution.py:25
  651.1 8.8 %fusion.23 = f32[1024,512]{1,0:T(8,128)S(1)} fusion(bf16[1024,8192]{1,0:T(8,128)(2,1)} %all-gather.7.cloned.1.call-done, s32[]{:T(128)S(6)} %select_n.100, bf16[1024,512]{1,0:T(8,128)(2,1)} %get-tuple-element.29, bf16[1024,512]{1,0:T(8,128)(2,1)} %get-tuple-element.31, bf16[1024,512]{1,0:T(8,128)(2,1)} %get-tuple-element.33, ...), kind=kOutput, calls=%fused_computation.28 | convolution fusion | flops 4311744512 | bytes 14680068 | tf_op jit(solution)/shard_map/dot_general | solution.py:25
  660.0 10.0 %fusion.15 = f32[1024,512]{1,0:T(8,128)} fusion(bf16[1024,8192]{1,0:T(8,128)(2,1)} %all-gather.9.cloned.1.call-done, s32[]{:T(128)S(6)} %select_n.100, bf16[1024,512]{1,0:T(8,128)(2,1)} %get-tuple-element.29, bf16[1024,512]{1,0:T(8,128)(2,1)} %get-tuple-element.31, bf16[1024,512]{1,0:T(8,128)(2,1)} %get-tuple-element.33, ...), kind=kOutput, calls=%fused_computation.20 | convolution fusion | flops 4311744512 | bytes 14680068 | tf_op jit(solution)/shard_map/dot_general | solution.py:25
  670.0 10.1 %fusion.7 = f32[1024,512]{1,0:T(8,128)} fusion(bf16[1024,8192]{1,0:T(8,128)(2,1)} %all-gather.11.cloned.1.call-done, s32[]{:T(128)S(6)} %select_n.100, bf16[1024,512]{1,0:T(8,128)(2,1)} %get-tuple-element.29, bf16[1024,512]{1,0:T(8,128)(2,1)} %get-tuple-element.31, bf16[1024,512]{1,0:T(8,128)(2,1)} %get-tuple-element.33, ...), kind=kOutput, calls=%fused_computation.12 | convolution fusion | flops 4311744512 | bytes 14680068 | tf_op jit(solution)/shard_map/dot_general | solution.py:25
  684.2 8.6 %fusion.27 = f32[1024,512]{1,0:T(8,128)S(1)} fusion(bf16[4096,512]{1,0:T(8,128)(2,1)S(1)} %constant_dynamic-update-slice_fusion, bf16[1024,8192]{1,0:T(8,128)(2,1)} %all-gather.5.cloned.1.call-done, s32[]{:T(128)S(6)} %select_n.101), kind=kOutput, calls=%fused_computation.32 | convolution fusion | flops 4294967296 | bytes 14680068 | tf_op jit(solution)/shard_map/dot_general | solution.py:25
  692.9 3.1 multiply_reduce_fusion.7
  696.0 7.1 fusion.19
  703.1 3.2 multiply_reduce_fusion.6
  707.6 8.3 %fusion.11 = f32[1024,512]{1,0:T(8,128)S(1)} fusion(bf16[4096,512]{1,0:T(8,128)(2,1)} %copy-done.24, bf16[1024,8192]{1,0:T(8,128)(2,1)} %all-gather.9.cloned.1.call-done, s32[]{:T(128)S(6)} %select_n.101), kind=kOutput, calls=%fused_computation.16 | convolution fusion | flops 4294967296 | bytes 14680068 | tf_op jit(solution)/shard_map/dot_general | solution.py:25
  715.9 3.1 multiply_reduce_fusion.5
  719.6 8.3 %fusion.3 = f32[1024,512]{1,0:T(8,128)S(1)} fusion(bf16[4096,512]{1,0:T(8,128)(2,1)} %copy-done.24, bf16[1024,8192]{1,0:T(8,128)(2,1)} %all-gather.11.cloned.1.call-done, s32[]{:T(128)S(6)} %select_n.101), kind=kOutput, calls=%fused_computation.8 | convolution fusion | flops 4294967296 | bytes 14680068 | tf_op jit(solution)/shard_map/dot_general | solution.py:25
  728.0 3.1 multiply_reduce_fusion.4
  742.6 3.5 collective-permute-done.16
  747.7 2.9 collective-permute-done.17
  752.6 14.1 %fusion = (f32[4096,512]{1,0:T(8,128)}, f32[4096,512]{1,0:T(8,128)}) fusion(f32[1024,512]{1,0:T(8,128)} %get-tuple-element.42, f32[1024,512]{1,0:T(8,128)} %get-tuple-element.41, f32[1024,512]{1,0:T(8,128)} %get-tuple-element.40, f32[1024,512]{1,0:T(8,128)} %get-tuple-element.39, f32[1024,512]{1,0:T(8,128)} %get-tuple-element.30, ...), kind=kLoop, calls=%fused_computation.2 | loop fusion | flops 20971520 | bytes 41943044 | tf_op jit(solution)/shard_map/sub | solution.py:138
  (130 shorter events, 42.3 us)
Async XLA Ops:
  8.0 178.9 %reduce-scatter.2.cloned.1.call-start = ((), (), s32[]{:S(2)}) async-start(), calls=%async_computation.1 | async-start | bytes 4718592 | tf_op jit(solution)/shard_map/reduce_scatter | solution.py:62
  18.6 440.8 %all-gather.7.cloned.1.call-start = ((), (), s32[]{:S(2)}) async-start(), calls=%async_computation.3 | async-start | bytes 17825792 | tf_op jit(solution)/shard_map/all_gather | solution.py:94
  24.8 458.5 %all-gather.9.cloned.1.call-start = ((), (), s32[]{:S(2)}) async-start(), calls=%async_computation.4 | async-start | bytes 17825792 | tf_op jit(solution)/shard_map/all_gather | solution.py:94
  25.4 480.0 %all-gather.11.cloned.1.call-start = ((), (), s32[]{:S(2)}) async-start(), calls=%async_computation.5 | async-start | bytes 17825792 | tf_op jit(solution)/shard_map/all_gather | solution.py:94
  25.9 593.4 %all-gather.5.cloned.1.call-start = ((), (), s32[]{:S(2)}) async-start(), calls=%async_computation.2 | async-start | bytes 17825792 | tf_op jit(solution)/shard_map/all_gather | solution.py:94
  188.2 2.0 collective-permute-start
  190.3 11.8 %collective-permute-start.1 = (bf16[256,512]{1,0:T(8,128)(2,1)S(1)}, bf16[256,512]{1,0:T(8,128)(2,1)S(1)}, u32[]{:S(2)}, u32[]{:S(2)}) collective-permute-start(bf16[256,512]{1,0:T(8,128)(2,1)S(1)} %constant_dynamic-slice_fusion), channel_id=1, source_target_pairs={{0,2},{2,0},{4,6},{6,4},{8,10},{10,8},{12,14},{14,12},{1,3},{3,1},... | collective-permute-start | bytes 786440 | tf_op jit(solution)/shard_map/ppermute | solution.py:16
  202.2 31.2 %collective-permute-start.2 = (bf16[256,1024]{1,0:T(8,128)(2,1)S(1)}, bf16[256,1024]{1,0:T(8,128)(2,1)S(1)}, u32[]{:S(2)}, u32[]{:S(2)}) collective-permute-start(bf16[256,1024]{1,0:T(8,128)(2,1)S(1)} %maximum_select_fusion.2), channel_id=1, source_target_pairs={{0,4},{2,6},{4,0},{6,2},{8,12},{10,14},{12,8},{14,10},{1,5},{3,7},... | collective-permute-start | bytes 1572872 | tf_op jit(solution)/shard_map/ppermute | solution.py:16
  233.8 103.7 %collective-permute-start.3 = (bf16[256,2048]{1,0:T(8,128)(2,1)S(1)}, bf16[256,2048]{1,0:T(8,128)(2,1)}, u32[]{:S(2)}, u32[]{:S(2)}) collective-permute-start(bf16[256,2048]{1,0:T(8,128)(2,1)S(1)} %maximum_select_fusion.1), channel_id=1, source_target_pairs={{0,8},{2,10},{4,12},{6,14},{8,0},{10,2},{12,4},{14,6},{1,9},{3,11}... | collective-permute-start | bytes 3145736 | tf_op jit(solution)/shard_map/ppermute | solution.py:16
  340.4 12.1 %copy-start.16 = (bf16[256,4096]{1,0:T(8,128)(2,1)}, bf16[256,4096]{1,0:T(8,128)(2,1)S(1)}, u32[]{:S(2)}) copy-start(bf16[256,4096]{1,0:T(8,128)(2,1)S(1)} %maximum_select_fusion) | copy-start | bytes 6291460
  340.4 23.0 %collective-permute-start.4 = (bf16[256,4096]{1,0:T(8,128)(2,1)S(1)}, bf16[256,4096]{1,0:T(8,128)(2,1)}, u32[]{:S(2)}, u32[]{:S(2)}) collective-permute-start(bf16[256,4096]{1,0:T(8,128)(2,1)S(1)} %maximum_select_fusion), channel_id=1, source_target_pairs={{0,16},{16,0},{1,17},{17,1},{2,18},{18,2},{3,19},{19,3},{4,20},{20... | collective-permute-start | bytes 6291464 | tf_op jit(solution)/shard_map/ppermute | solution.py:72
  341.7 21.5 %collective-permute-start.5 = (bf16[2,512,512]{2,1,0:T(8,128)(2,1)}, bf16[2,512,512]{2,1,0:T(8,128)(2,1)}, u32[]{:S(2)}, u32[]{:S(2)}) collective-permute-start(bf16[2,512,512]{2,1,0:T(8,128)(2,1)} %pad_maximum_fusion.6), channel_id=1, source_target_pairs={{0,1},{17,16},{2,3},{19,18},{4,5},{21,20},{6,7},{23,22},{8,9},{25,... | collective-permute-start | bytes 3145736 | tf_op jit(solution)/shard_map/ppermute | solution.py:68
  352.5 115.6 %collective-permute-start.6 = (bf16[4096,512]{1,0:T(8,128)(2,1)}, bf16[4096,512]{1,0:T(8,128)(2,1)}, u32[]{:S(2)}, u32[]{:S(2)}) collective-permute-start(bf16[4096,512]{1,0:T(8,128)(2,1)} %convert_element_type.57), channel_id=1, source_target_pairs={{0,1},{1,0},{2,3},{3,2},{4,5},{5,4},{6,7},{7,6},{8,9},{9,8},{10,11... | collective-permute-start | bytes 12582920 | tf_op jit(solution)/shard_map/ppermute | solution.py:34
  352.5 10.9 %copy-start.17 = (bf16[256,4096]{1,0:T(8,128)(2,1)S(1)}, bf16[256,4096]{1,0:T(8,128)(2,1)}, u32[]{:S(2)}) copy-start(bf16[256,4096]{1,0:T(8,128)(2,1)} %copy-done.16) | copy-start | bytes 6291460
  363.4 11.9 %slice-start = ((s8[8388608]{0:T(1024)(128)(4,1)}), s8[4194304]{0:T(1024)(128)(4,1)S(1)}, s32[]{:S(2)}) async-start(s8[8388608]{0:T(1024)(128)(4,1)} %bitcast.57), calls=%async_computation.6 | async-start | bytes 8388608
  365.7 19.5 %copy-start.2 = (bf16[256,4096]{1,0:T(8,128)(2,1)}, bf16[256,4096]{1,0:T(8,128)(2,1)S(1)}, u32[]{:S(2)}) copy-start(bf16[256,4096]{1,0:T(8,128)(2,1)S(1)} %get-tuple-element.22) | copy-start | bytes 6291460
  365.7 9.6 %slice-start.1 = ((s8[8388608]{0:T(1024)(128)(4,1)}), s8[4194304]{0:T(1024)(128)(4,1)S(1)}, s32[]{:S(2)}) async-start(s8[8388608]{0:T(1024)(128)(4,1)} %bitcast.57), calls=%async_computation.7 | async-start | bytes 8388608
  371.4 9.0 %slice-start.2 = ((s8[8388608]{0:T(1024)(128)(4,1)}), s8[4194304]{0:T(1024)(128)(4,1)S(1)}, s32[]{:S(2)}) async-start(s8[8388608]{0:T(1024)(128)(4,1)} %bitcast.61), calls=%async_computation.8 | async-start | bytes 8388608
  371.4 9.0 %slice-start.3 = ((s8[8388608]{0:T(1024)(128)(4,1)}), s8[4194304]{0:T(1024)(128)(4,1)S(1)}, s32[]{:S(2)}) async-start(s8[8388608]{0:T(1024)(128)(4,1)} %bitcast.61), calls=%async_computation.9 | async-start | bytes 8388608
  371.4 87.8 %collective-permute-start.7 = (bf16[512,512]{1,0:T(8,128)(2,1)S(1)}, bf16[512,512]{1,0:T(8,128)(2,1)S(1)}, u32[]{:S(2)}, u32[]{:S(2)}) collective-permute-start(bf16[512,512]{1,0:T(8,128)(2,1)S(1)} %get-tuple-element.27), channel_id=1, source_target_pairs={{0,1},{1,0},{2,3},{3,2},{4,5},{5,4},{6,7},{7,6},{8,9},{9,8},{10,11... | collective-permute-start | bytes 1572872 | tf_op jit(solution)/shard_map/ppermute | solution.py:34
  459.5 9.9 %copy-start.27 = (bf16[1024,8192]{1,0:T(8,128)(2,1)S(1)}, bf16[1024,8192]{1,0:T(8,128)(2,1)}, u32[]{:S(2)}) copy-start(bf16[1024,8192]{1,0:T(8,128)(2,1)} %all-gather.7.cloned.1.call-done) | copy-start | bytes 50331652
  468.1 7.8 %copy-start.13 = (bf16[512,1024]{1,0:T(8,128)(2,1)S(1)}, bf16[512,1024]{1,0:T(8,128)(2,1)}, u32[]{:S(2)}) copy-start(bf16[512,1024]{1,0:T(8,128)(2,1)} %get-tuple-element.18) | copy-start | bytes 3145732
  481.0 199.4 %collective-permute-start.9 = (bf16[1024,512]{1,0:T(8,128)(2,1)}, bf16[1024,512]{1,0:T(8,128)(2,1)}, u32[]{:S(2)}, u32[]{:S(2)}) collective-permute-start(bf16[1024,512]{1,0:T(8,128)(2,1)} %get-tuple-element.33), channel_id=1, source_target_pairs={{0,1},{1,0},{2,3},{3,2},{4,5},{5,4},{6,7},{7,6},{8,9},{9,8},{10,11... | collective-permute-start | bytes 3145736 | tf_op jit(solution)/shard_map/ppermute | solution.py:34
  483.3 10.3 %copy-start.26 = (bf16[1024,8192]{1,0:T(8,128)(2,1)S(1)}, bf16[1024,8192]{1,0:T(8,128)(2,1)}, u32[]{:S(2)}) copy-start(bf16[1024,8192]{1,0:T(8,128)(2,1)} %all-gather.9.cloned.1.call-done) | copy-start | bytes 50331652
  505.3 176.4 %collective-permute-start.10 = (bf16[1024,512]{1,0:T(8,128)(2,1)}, bf16[1024,512]{1,0:T(8,128)(2,1)}, u32[]{:S(2)}, u32[]{:S(2)}) collective-permute-start(bf16[1024,512]{1,0:T(8,128)(2,1)} %get-tuple-element.31), channel_id=1, source_target_pairs={{0,1},{1,0},{2,3},{3,2},{4,5},{5,4},{6,7},{7,6},{8,9},{9,8},{10,11... | collective-permute-start | bytes 3145736 | tf_op jit(solution)/shard_map/ppermute | solution.py:34
  505.4 9.5 %copy-start.25 = (bf16[1024,8192]{1,0:T(8,128)(2,1)S(1)}, bf16[1024,8192]{1,0:T(8,128)(2,1)}, u32[]{:S(2)}) copy-start(bf16[1024,8192]{1,0:T(8,128)(2,1)} %all-gather.11.cloned.1.call-done) | copy-start | bytes 50331652
  521.5 7.3 copy-start.14
  521.5 10.2 %copy-start.11 = (bf16[512,1024]{1,0:T(8,128)(2,1)S(1)}, bf16[512,1024]{1,0:T(8,128)(2,1)}, u32[]{:S(2)}) copy-start(bf16[512,1024]{1,0:T(8,128)(2,1)} %get-tuple-element.19) | copy-start | bytes 3145732
  526.8 156.1 %collective-permute-start.11 = (bf16[1024,512]{1,0:T(8,128)(2,1)}, bf16[1024,512]{1,0:T(8,128)(2,1)}, u32[]{:S(2)}, u32[]{:S(2)}) collective-permute-start(bf16[1024,512]{1,0:T(8,128)(2,1)} %get-tuple-element.29), channel_id=1, source_target_pairs={{0,1},{1,0},{2,3},{3,2},{4,5},{5,4},{6,7},{7,6},{8,9},{9,8},{10,11... | collective-permute-start | bytes 3145736 | tf_op jit(solution)/shard_map/ppermute | solution.py:34
  619.3 9.4 %copy-start.28 = (bf16[1024,8192]{1,0:T(8,128)(2,1)S(1)}, bf16[1024,8192]{1,0:T(8,128)(2,1)}, u32[]{:S(2)}) copy-start(bf16[1024,8192]{1,0:T(8,128)(2,1)} %all-gather.5.cloned.1.call-done) | copy-start | bytes 50331652
  639.0 53.9 %copy-start.7 = (f32[1024,512]{1,0:T(8,128)}, f32[1024,512]{1,0:T(8,128)S(1)}, u32[]{:S(2)}) copy-start(f32[1024,512]{1,0:T(8,128)S(1)} %get-tuple-element.36) | copy-start | bytes 6291460
  639.0 41.3 %collective-permute-start.8 = (bf16[1024,512]{1,0:T(8,128)(2,1)S(1)}, bf16[1024,512]{1,0:T(8,128)(2,1)S(1)}, u32[]{:S(2)}, u32[]{:S(2)}) collective-permute-start(bf16[1024,512]{1,0:T(8,128)(2,1)S(1)} %get-tuple-element.35), channel_id=1, source_target_pairs={{0,1},{1,0},{2,3},{3,2},{4,5},{5,4},{6,7},{7,6},{8,9},{9,8},{10,11... | collective-permute-start | bytes 3145736 | tf_op jit(solution)/shard_map/ppermute | solution.py:34
  641.2 38.8 %collective-permute-start.12 = (bf16[512,512]{1,0:T(8,128)(2,1)S(1)}, bf16[512,512]{1,0:T(8,128)(2,1)S(1)}, u32[]{:S(2)}, u32[]{:S(2)}) collective-permute-start(bf16[512,512]{1,0:T(8,128)(2,1)S(1)} %get-tuple-element.37), channel_id=1, source_target_pairs={{0,1},{1,0},{2,3},{3,2},{4,5},{5,4},{6,7},{7,6},{8,9},{9,8},{10,11... | collective-permute-start | bytes 1572872 | tf_op jit(solution)/shard_map/ppermute | solution.py:34
  684.2 11.7 %copy-start.24 = (bf16[4096,512]{1,0:T(8,128)(2,1)}, bf16[4096,512]{1,0:T(8,128)(2,1)S(1)}, u32[]{:S(2)}) copy-start(bf16[4096,512]{1,0:T(8,128)(2,1)S(1)} %constant_dynamic-update-slice_fusion) | copy-start | bytes 12582916
  696.0 7.1 copy-start.4
  696.0 7.1 copy-start.15
  707.5 8.3 %copy-start.5 = (f32[1024,512]{1,0:T(8,128)S(1)}, f32[1024,512]{1,0:T(8,128)}, u32[]{:S(2)}) copy-start(f32[1024,512]{1,0:T(8,128)} %get-tuple-element.32) | copy-start | bytes 6291460
  707.5 8.3 %copy-start.12 = (bf16[512,1024]{1,0:T(8,128)(2,1)S(1)}, bf16[512,1024]{1,0:T(8,128)(2,1)}, u32[]{:S(2)}) copy-start(bf16[512,1024]{1,0:T(8,128)(2,1)} %get-tuple-element.19) | copy-start | bytes 3145732
  707.5 8.3 %copy-start.20 = (f32[1024,512]{1,0:T(8,128)S(1)}, f32[1024,512]{1,0:T(8,128)}, u32[]{:S(2)}) copy-start(f32[1024,512]{1,0:T(8,128)} %fusion.15) | copy-start | bytes 6291460
  719.6 8.3 %copy-start.6 = (f32[1024,512]{1,0:T(8,128)S(1)}, f32[1024,512]{1,0:T(8,128)}, u32[]{:S(2)}) copy-start(f32[1024,512]{1,0:T(8,128)} %get-tuple-element.30) | copy-start | bytes 6291460
  719.6 8.3 %copy-start.9 = (bf16[512,1024]{1,0:T(8,128)(2,1)S(1)}, bf16[512,1024]{1,0:T(8,128)(2,1)}, u32[]{:S(2)}) copy-start(bf16[512,1024]{1,0:T(8,128)(2,1)} %get-tuple-element.20) | copy-start | bytes 3145732
  719.6 8.3 %copy-start.19 = (f32[1024,512]{1,0:T(8,128)S(1)}, f32[1024,512]{1,0:T(8,128)}, u32[]{:S(2)}) copy-start(f32[1024,512]{1,0:T(8,128)} %fusion.7) | copy-start | bytes 6291460
  734.3 1.1 collective-permute-start.13
  735.5 3.5 collective-permute-start.14
  739.1 3.5 collective-permute-start.15
  742.6 3.5 collective-permute-start.16
  746.2 4.4 collective-permute-start.17
  752.6 14.1 %copy-start.1 = (bf16[1,512,1024]{2,1,0:T(8,128)(2,1)S(1)}, bf16[1,512,1024]{2,1,0:T(8,128)(2,1)}, u32[]{:S(2)}) copy-start(bf16[1,512,1024]{2,1,0:T(8,128)(2,1)} %param.6) | copy-start | bytes 3145732
  (8 other events, 39.0 us)
Sparse Core Ops, SparseCore 0:
  18.8 168.0 reduce-scatter.1
Sparse Core Ops, SparseCore 1:
  24.8 147.6 all-gather.6
  174.7 179.9 all-gather.8
  356.8 132.0 all-gather.10
  491.1 128.1 all-gather.4
